TPU v7x, 32 devices: a whole 2x2x4 slice. The times are simulated.
32 devices in a mesh: parts: 2 (over x), chol: 16 (over z, y, core).
Axes of the slice: x: 2, y: 2, z: 4, core: 2. Of those that a mesh axis runs over, the one named last changes fastest.
Arguments:
- walkers: bfloat16 [32, 2304, 320], P(('parts', 'chol')), parts along dimension 0, may hold values from -6 to 6
- left_factor: bfloat16 [32, 320, 2304], P(('parts', 'chol')), parts along dimension 0, may hold values from -0.3125 to 0.3125
- chol_tiles: bfloat16 [64, 48, 16384], P('chol'), may hold values from -0.046875 to 0.046875
- tile_block: int32 [64], replicated, may hold values from 0 to 323
- fields: float32 [32, 3072], P('parts', 'chol'), parts along dimension 0, may hold values from -6 to 6
Outputs:
- force_bias: float32 [32, 3072], P('parts', 'chol'), parts along dimension 0
- new_walkers: bfloat16 [32, 2304, 320], P(('parts', 'chol')), parts along dimension 0
There are 2 independent parts, one for each index of `parts`. A program takes and returns all parts, laid end to end along the dimension named above; an argument that names none is the same for every part. Nothing has to cross between parts.
All inputs are finite; a program needn't handle non-finite values.
Results may differ from a plain program's by a relative error of at most 0.0051.
Values may be sent and summed in bfloat16 or wider, within the bound.
A program may use at most 128 MiB of HBM per device.

v0:
```python
import jax
import jax.numpy as jnp
from jax import lax
from jax.sharding import PartitionSpec as P

BS = 128


step_root = 0.25


def per_device(walkers, left_factor, chol_tiles, tile_block, fields):
    local_walkers, orbital_count, occupied = walkers.shape
    tile_count, vector_count, area = chol_tiles.shape
    block_size = BS
    blocks_side = orbital_count // block_size
    all_tiles = tile_block.shape[0]
    rows_all = walkers.reshape(local_walkers, blocks_side, block_size, occupied)
    cols_all = left_factor.reshape(local_walkers, occupied, blocks_side, block_size)
    grouped = tile_block.reshape(-1, 8 * tile_count)

    def build(blocks):
        rows = jnp.take(rows_all, blocks // blocks_side, axis=1)
        cols = jnp.take(cols_all, blocks % blocks_side, axis=2)
        green = jnp.einsum("wtie,wetk->wtik", rows, cols, preferred_element_type=jnp.float32)
        return green.astype(jnp.bfloat16).reshape(local_walkers, blocks.shape[0], area)

    built = lax.map(build, grouped)
    built = built.transpose(1, 0, 2, 3).reshape(local_walkers, all_tiles, area)
    received = lax.all_to_all(built, "chol", split_axis=1, concat_axis=0, tiled=True)
    walker_count = received.shape[0]
    field_tiles = fields.reshape(walker_count, tile_count, vector_count)
    bias = jnp.einsum("wje,jge->wjg", received, chol_tiles, preferred_element_type=jnp.float32)
    shifted = (field_tiles + bias).astype(jnp.bfloat16)
    parts = jnp.einsum(
        "wjg,jge->wje", shifted, chol_tiles, preferred_element_type=jnp.float32
    ).astype(jnp.bfloat16)
    force_bias = bias.reshape(walker_count, tile_count * vector_count)
    returned = lax.all_to_all(parts, "chol", split_axis=0, concat_axis=1, tiled=True)

    def propagate(items):
        orbitals, pieces = items
        summed = jax.ops.segment_sum(
            pieces.astype(jnp.float32), tile_block, num_segments=blocks_side * blocks_side
        )
        whole = summed.reshape(blocks_side, blocks_side, block_size, block_size).transpose(
            0, 2, 1, 3
        )
        operator = (-step_root * whole.reshape(orbital_count, orbital_count)).astype(jnp.bfloat16)
        term = orbitals
        total = orbitals.astype(jnp.float32)
        for order in range(1, 4):
            term = (jnp.dot(operator, term, preferred_element_type=jnp.float32) / order).astype(
                jnp.bfloat16
            )
            total = total + term.astype(jnp.float32)
        return total.astype(jnp.bfloat16)

    new_walkers = lax.map(propagate, (walkers, returned))
    return (force_bias, new_walkers)


def solution(mesh):
    in_specs = (
        P(("parts", "chol"), None, None),
        P(("parts", "chol"), None, None),
        P("chol", None, None),
        P(),
        P("parts", "chol"),
    )
    out_specs = (P("parts", "chol"), P(("parts", "chol"), None, None))
    return jax.shard_map(
        per_device, mesh=mesh, in_specs=in_specs, out_specs=out_specs, check_vma=False
    )
```

profile of v0, /device:TPU:13, one launch (start us, length us, event | category | flops | bytes accessed | tf_op | source)
XLA Modules:
  0.0 253.7 jit_solution(11592936344384592840)
XLA Ops:
  0.6 0.7 reshape.181
  1.4 2.7 %copy.38 = bf16[1,320,2304]{1,2,0:T(8,128)(2,1)S(1)} copy(bf16[1,320,2304]{2,1,0:T(8,128)(2,1)} %param.8) | data formatting | bytes 2949120 | tf_op args[1]
  4.1 1.1 copy.39
  5.2 2.7 %copy.37 = bf16[1,2304,320]{2,1,0:T(8,128)(2,1)S(1)} copy(bf16[1,2304,320]{1,2,0:T(8,128)(2,1)} %param.7) | data formatting | bytes 2949120 | tf_op args[0]
  7.9 28.9 %while.16 = (s32[]{:T(128)}, bf16[2,1,32,16384]{3,2,1,0:T(8,128)(2,1)}, s32[2,32]{1,0:T(2,128)S(1)}, bf16[1,18,128,320]{3,2,1,0:T(8,128)(2,1)S(1)}, bf16[1,320,18,128]{3,1,2,0:T(8,128)(2,1)S(1)}, /*index=5*/s32[]{:T(128)}) while((s32[]{:T(128)}, bf16[2,1,32,16384]{3,2,1,0:T(8,128)(2,1)}, s32[2,32]{1,0:T(2,128)S(1)}, ...), condition=%wide.region_1.2_spmd, body=%wide.region_0.1_spmd.sunk | while | flops 338693472 | bytes 20981460 | solution.py:28
  8.0 2.4 gather_fusion
  10.4 2.6 %gather_fusion.1 = bf16[32,128,320]{2,1,0:T(8,128)(2,1)} fusion(bf16[18,128,320]{2,1,0:T(8,128)(2,1)S(1)} %bitcast.119, s32[1024]{0:T(1024)S(1)} %get-tuple-element.166), kind=kCustom, calls=%fused_computation.clone.1 | custom fusion | bytes 5243008 | tf_op jit(solution)/shard_map/while/body/eval_jaxpr/jit(_take)/gather | solution.py:23
  13.1 4.7 %fusion.76 = bf16[32,128,128]{2,1,0:T(8,128)(2,1)} fusion(bf16[32,320,128]{2,1,0:T(8,128)(2,1)} %gather_fusion, pred[32]{0:T(512)(128)(4,1)S(1)} %compare_and_fusion.5, bf16[32,128,320]{2,1,0:T(8,128)(2,1)} %gather_fusion.1, pred[32]{0:T(512)(128)(4,1)S(1)} %get-tuple-element.167), kind=kOutput, calls=%fused_computation.10.clone.1 | convolution fusion | flops 338690048 | bytes 6291520 | tf_op jit(solution)/shard_map/while/body/eval_jaxpr/wtie,wetk->wtik/dot_general | solution.py:25
  17.8 2.3 broadcast_in_dim.60
  20.1 2.3 constant_dynamic-update-slice_fusion.2
  22.5 2.4 gather_fusion
  24.9 2.6 %gather_fusion.1 = bf16[32,128,320]{2,1,0:T(8,128)(2,1)} fusion(bf16[18,128,320]{2,1,0:T(8,128)(2,1)S(1)} %bitcast.119, s32[1024]{0:T(1024)S(1)} %get-tuple-element.166), kind=kCustom, calls=%fused_computation.clone.1 | custom fusion | bytes 5243008 | tf_op jit(solution)/shard_map/while/body/eval_jaxpr/jit(_take)/gather | solution.py:23
  27.5 4.7 %fusion.76 = bf16[32,128,128]{2,1,0:T(8,128)(2,1)} fusion(bf16[32,320,128]{2,1,0:T(8,128)(2,1)} %gather_fusion, pred[32]{0:T(512)(128)(4,1)S(1)} %compare_and_fusion.5, bf16[32,128,320]{2,1,0:T(8,128)(2,1)} %gather_fusion.1, pred[32]{0:T(512)(128)(4,1)S(1)} %get-tuple-element.167), kind=kOutput, calls=%fused_computation.10.clone.1 | convolution fusion | flops 338690048 | bytes 6291520 | tf_op jit(solution)/shard_map/while/body/eval_jaxpr/wtie,wetk->wtik/dot_general | solution.py:25
  32.2 2.3 broadcast_in_dim.60
  34.5 2.2 constant_dynamic-update-slice_fusion.2
  36.8 8.2 %copy.89 = bf16[1,64,16384]{2,0,1:T(2,128)(2,1)} copy(bf16[1,64,16384]{2,1,0:T(8,128)(2,1)} %bitcast.131) | data formatting | bytes 4194304 | tf_op jit(solution)/shard_map/reshape;transpose | solution.py:29
  45.0 0.5 broadcast.298
  45.5 13.2 %reduce.2 = bf16[64,16384]{1,0:T(8,128)(2,1)S(1)} reduce(bf16[64,1,16384]{2,1,0:T(2,128)(2,1)} %bitcast.126, bf16[]{:T(256)} %broadcast.298), dimensions={1}, to_apply=%bitcast.95.reduce_sub_computation | reduce | bytes 4194306
  58.6 2.8 %reshape.221 = bf16[16,2,32768]{2,1,0:T(2,128)(2,1)} reshape(bf16[64,16384]{1,0:T(8,128)(2,1)S(1)} %reduce.2) | data formatting | bytes 4194304
  61.4 0.0 copy-start.1
  61.5 6.7 %all-to-all-start = ((bf16[16,2,32768]{2,1,0:T(2,128)(2,1)}), bf16[16,2,32768]{2,1,0:T(2,128)(2,1)S(1)}, u32[]{:S(2)}, u32[]{:S(2)}) async-start(bf16[16,2,32768]{2,1,0:T(2,128)(2,1)} %reshape.221), calls=%async_computation | async-start | bytes 4194304 | tf_op jit(solution)/shard_map/all_to_all | solution.py:30
  68.1 0.0 copy-done.1
  68.1 0.1 reshape.185
  68.2 47.3 %all-to-all-done = bf16[16,2,32768]{2,1,0:T(2,128)(2,1)S(1)} async-done(((bf16[16,2,32768]{2,1,0:T(2,128)(2,1)}), bf16[16,2,32768]{2,1,0:T(2,128)(2,1)S(1)}, u32[]{:S(2)}, u32[]{:S(2)}) %all-to-all-start) | async-done | bytes 2097184 | tf_op jit(solution)/shard_map/all_to_all | solution.py:30
  115.6 6.7 %reshape.222 = bf16[64,1,16384]{2,1,0:T(2,128)(2,1)} reshape(bf16[16,2,32768]{2,1,0:T(2,128)(2,1)S(1)} %all-to-all-done) | data formatting | bytes 4194304
  122.2 14.2 %bitcast_reduce_fusion = bf16[64,16384]{1,0:T(8,128)(2,1)} fusion(bf16[64,1,16384]{2,1,0:T(2,128)(2,1)} %reshape.222), kind=kLoop, calls=%fused_computation.62 | loop fusion | bytes 4194304 | tf_op jit(solution)/shard_map/all_to_all | solution.py:30
  136.4 0.0 slice-start
  136.4 4.2 %all_to_all.7 = bf16[16,4,16384]{2,1,0:T(4,128)(2,1)} reshape(bf16[64,16384]{1,0:T(8,128)(2,1)} %bitcast_reduce_fusion) | data formatting | bytes 4194304 | tf_op jit(solution)/shard_map/all_to_all | solution.py:30
  140.6 0.0 slice-start.1
  140.6 5.5 %fusion.60 = f32[16,4,48]{2,0,1:T(8,128)S(1)} fusion(bf16[4,48,16384]{2,1,0:T(8,128)(2,1)} %param.9, bf16[16,4,16384]{2,1,0:T(4,128)(2,1)} %all_to_all.7), kind=kOutput, calls=%fused_computation.59 | convolution fusion | flops 100663296 | bytes 8400896 | tf_op jit(solution)/shard_map/wje,jge->wjg/dot_general | solution.py:33
  146.2 0.0 slice-done
  146.2 0.0 slice-done.1
  146.2 1.0 fusion.18
  147.1 3.0 %copy.44 = bf16[16,4,16384]{2,1,0:T(4,128)(2,1)} copy(bf16[16,4,16384]{2,0,1:T(8,128)(2,1)S(1)} %fusion.18) | data formatting | bytes 4194304 | tf_op jit(solution)/shard_map/convert_element_type | solution.py:37
  150.1 4.9 %all-to-all-start.1 = ((bf16[16,4,16384]{2,1,0:T(4,128)(2,1)}), bf16[16,4,16384]{2,1,0:T(4,128)(2,1)S(1)}, u32[]{:S(2)}, u32[]{:S(2)}) async-start(bf16[16,4,16384]{2,1,0:T(4,128)(2,1)} %copy.44), calls=%async_computation.1 | async-start | bytes 4194304 | tf_op jit(solution)/shard_map/all_to_all | solution.py:39
  155.0 0.7 reshape.184
  155.7 46.7 %all-to-all-done.1 = bf16[16,4,16384]{2,1,0:T(4,128)(2,1)S(1)} async-done(((bf16[16,4,16384]{2,1,0:T(4,128)(2,1)}), bf16[16,4,16384]{2,1,0:T(4,128)(2,1)S(1)}, u32[]{:S(2)}, u32[]{:S(2)}) %all-to-all-start.1) | async-done | bytes 2097184 | tf_op jit(solution)/shard_map/all_to_all | solution.py:39
  202.4 2.6 %reshape.211 = f32[64,16384]{1,0:T(8,128)} reshape(bf16[16,4,16384]{2,1,0:T(4,128)(2,1)S(1)} %all-to-all-done.1) | data formatting | bytes 6291456 | tf_op jit(solution)/shard_map/while/body/eval_jaxpr/convert_element_type | solution.py:44
  205.0 15.3 %scatter_custom_fusion = f32[324,16384]{1,0:T(8,128)} fusion(s32[64]{0:T(128)} %param.10, f32[64,16384]{1,0:T(8,128)} %reshape.211, f32[]{:T(128)} %constant.101.clone.1), kind=kCustom, calls=%fused_computation.36 | custom fusion | flops 1048576 | bytes 21234176 | tf_op jit(solution)/shard_map/while/body/eval_jaxpr/scatter-add | solution.py:43
  220.3 8.2 %multiply_convert_fusion = bf16[324,16384]{1,0:T(8,128)(2,1)S(1)} fusion(f32[324,16384]{1,0:T(8,128)} %scatter_custom_fusion), kind=kLoop, calls=%fused_computation.33 | loop fusion | flops 10616832 | bytes 31850496 | tf_op jit(solution)/shard_map/while/body/eval_jaxpr/convert_element_type | solution.py:49
  228.5 2.1 copy.48
  230.6 0.8 slice.4
  231.5 0.0 copy-start
  231.5 10.0 %copy.45 = bf16[18,128,18,128]{3,2,1,0:T(8,128)(2,1)S(1)} copy(bf16[18,128,18,128]{3,1,2,0:T(8,128)(2,1)S(1)} %bitcast.123) | data formatting | bytes 21233664 | tf_op jit(solution)/shard_map/while/body/eval_jaxpr/convert_element_type | solution.py:49
  241.5 0.0 copy-done
  241.5 3.6 %fusion.45 = bf16[2304,320]{0,1:T(8,128)(2,1)S(1)} fusion(bf16[288,8,18,128]{3,2,1,0:T(8,128)(2,1)S(1)} %bitcast.127, bf16[1,2304,320]{1,2,0:T(8,128)(2,1)S(1)} %copy-done), kind=kOutput, calls=%fused_computation.52 | convolution fusion | flops 3398123520 | bytes 13565952 | tf_op jit(solution)/shard_map/while/body/eval_jaxpr/dot_general | solution.py:53
  245.2 3.6 %fusion.42 = bf16[2304,320]{0,1:T(8,128)(2,1)S(1)} fusion(bf16[2304,320]{0,1:T(8,128)(2,1)S(1)} %fusion.45, bf16[288,8,18,128]{3,2,1,0:T(8,128)(2,1)S(1)} %bitcast.128), kind=kOutput, calls=%fused_computation.51 | convolution fusion | flops 3398860800 | bytes 13565952 | tf_op jit(solution)/shard_map/while/body/eval_jaxpr/dot_general | solution.py:53
  248.8 4.8 %fusion.54 = bf16[1,2304,320]{1,2,0:T(8,128)(2,1)} fusion(bf16[2304,320]{0,1:T(8,128)(2,1)S(1)} %fusion.42, bf16[288,8,18,128]{3,2,1,0:T(8,128)(2,1)S(1)} %bitcast.129, bf16[2304,320]{0,1:T(8,128)(2,1)S(1)} %fusion.45, bf16[1,2304,320]{1,2,0:T(8,128)(2,1)S(1)} %copy-done), kind=kOutput, calls=%fused_computation.55 | convolution fusion | flops 3404759040 | bytes 16515072 | tf_op jit(solution)/shard_map/while/body/eval_jaxpr/dot_general | solution.py:53
  (11 shorter events, 0.1 us)
Async XLA Ops:
  61.4 6.7 %copy-start.1 = (f32[16,192]{1,0:T(8,128)S(1)}, f32[16,192]{1,0:T(8,128)}, u32[]{:S(2)}) copy-start(f32[16,192]{1,0:T(8,128)} %param.11) | copy-start | bytes 36868
  61.5 54.1 %all-to-all-start = ((bf16[16,2,32768]{2,1,0:T(2,128)(2,1)}), bf16[16,2,32768]{2,1,0:T(2,128)(2,1)S(1)}, u32[]{:S(2)}, u32[]{:S(2)}) async-start(bf16[16,2,32768]{2,1,0:T(2,128)(2,1)} %reshape.221), calls=%async_computation | async-start | bytes 4194304 | tf_op jit(solution)/shard_map/all_to_all | solution.py:30
  136.4 9.8 %slice-start = ((s8[6291456]{0:T(1024)(128)(4,1)}), s8[2097152]{0:T(1024)(128)(4,1)S(1)}, s32[]{:S(2)}) async-start(s8[6291456]{0:T(1024)(128)(4,1)} %bitcast.124), calls=%async_computation.2 | async-start | bytes 4194304
  140.6 5.5 %slice-start.1 = ((s8[6291456]{0:T(1024)(128)(4,1)}), s8[4194304]{0:T(1024)(128)(4,1)S(1)}, s32[]{:S(2)}) async-start(s8[6291456]{0:T(1024)(128)(4,1)} %bitcast.124), calls=%async_computation.3 | async-start | bytes 8388608
  150.1 52.3 %all-to-all-start.1 = ((bf16[16,4,16384]{2,1,0:T(4,128)(2,1)}), bf16[16,4,16384]{2,1,0:T(4,128)(2,1)S(1)}, u32[]{:S(2)}, u32[]{:S(2)}) async-start(bf16[16,4,16384]{2,1,0:T(4,128)(2,1)} %copy.44), calls=%async_computation.1 | async-start | bytes 4194304 | tf_op jit(solution)/shard_map/all_to_all | solution.py:39
  231.5 10.1 %copy-start = (bf16[1,2304,320]{1,2,0:T(8,128)(2,1)S(1)}, bf16[1,2304,320]{1,2,0:T(8,128)(2,1)}, u32[]{:S(2)}) copy-start(bf16[1,2304,320]{1,2,0:T(8,128)(2,1)} %param.7) | copy-start | bytes 4423684
where the time goes:
time: 254 us
  waiting for transfers between devices  94 us (37%)
  local copies, waits for them, and re-layouts  82.5 us (32%)
  other arithmetic  36.7 us (14%)
  matrix products  28 us (11%)
  starting transfers between devices  11.6 us (5%)
    all_to_all x1, waiting for transfers between devices, per_device(): lax.all_to_all(built, 'chol', split_axis=1, concat_axis=0, tiled=True)  47.3 us
    all_to_all x1, waiting for transfers between devices, per_device(): lax.all_to_all(parts, 'chol', split_axis=0, concat_axis=1, tiled=True)  46.7 us
    all_to_all x2, local copies, waits for them, and re-layouts, per_device(): lax.all_to_all(built, 'chol', split_axis=1, concat_axis=0, tiled=True)  18.4 us
    unnamed x15, local copies, waits for them, and re-layouts  18.4 us
    scatter-add x1, other arithmetic, propagate(): jax.ops.segment_sum(pieces.astype(jnp.float32), tile_block, num_segments=...  15.3 us
    unnamed x2, other arithmetic  13.2 us
    dot_general x3, matrix products, propagate(): jnp.dot(operator, term, preferred_element_type=jnp.float32) / order  12.1 us
    convert_element_type x1, local copies, waits for them, and re-layouts, propagate(): (-step_root * whole.reshape(orbital_count, orbital_count)).astype(jnp.bfl...  10 us
  transfers between devices with their start and end apart: 2, of which 2 were waited for; matrix products, arithmetic and copies ran while one was open for 0% of the time, Pallas kernels for 0%

commit v1 on v0

v1 whole, which is shorter than its diff:
```python
import functools

import jax
import jax.numpy as jnp
from jax import lax
from jax.experimental import pallas as pl
from jax.experimental.pallas import tpu as pltpu
from jax.sharding import PartitionSpec as P

BS = 128
MESH = pl.DeviceIdType.MESH

step_root = 0.25
CHUNK = 2048


def exchange_kernel(
    n,
    green,
    fields,
    chol_hbm,
    bias_out,
    returned,
    chol,
    received,
    back,
    wide,
    flat,
    field_tiles,
    bias_tiles,
    chol_sem,
    green_send,
    green_recv,
    back_send,
    back_recv,
    own_sem,
):
    me = lax.axis_index("chol")
    part = lax.axis_index("parts")
    tiles, vectors, area = chol.shape
    half = n // 2

    chol_copies = [
        pltpu.make_async_copy(chol_hbm.at[j], chol.at[j], chol_sem.at[j]) for j in range(tiles)
    ]
    for copy in chol_copies:
        copy.start()

    barrier = pltpu.get_barrier_semaphore()

    def greet(r, carry):
        pl.semaphore_signal(
            barrier, inc=1, device_id=(part, lax.rem(me + r, n)), device_id_type=MESH
        )
        return carry

    lax.fori_loop(1, n, greet, 0)

    for j in range(tiles):
        field_tiles[j] = fields[:, j * vectors : (j + 1) * vectors]

    def send_green(j, owner):
        t = owner * tiles + j
        pltpu.make_async_remote_copy(
            src_ref=green.at[t],
            dst_ref=received.at[j, me],
            send_sem=green_send,
            recv_sem=green_recv.at[j],
            device_id=(part, owner),
            device_id_type=MESH,
        ).start()

    for j in range(tiles):
        received[j, me] = green[me * tiles + j]
    pl.semaphore_wait(barrier, n - 1)

    def send_tile(j, carry):
        send_green(j, lax.rem(me + half, n))

        def pair(i, c):
            send_green(j, lax.rem(me + half + i, n))
            send_green(j, lax.rem(me + i, n))
            return c

        return lax.fori_loop(1, half, pair, carry)

    lax.fori_loop(0, tiles, send_tile, 0)

    def send_back(j, walker):
        pltpu.make_async_remote_copy(
            src_ref=back.at[j, walker],
            dst_ref=returned.at[me * tiles + j],
            send_sem=back_send,
            recv_sem=back_recv,
            device_id=(part, walker),
            device_id_type=MESH,
        ).start()

    def process(j, carry):
        arrived = received.at[j, pl.ds(0, n - 1)]
        pltpu.make_async_copy(arrived, arrived, green_recv.at[j]).wait()
        pltpu.make_async_copy(chol_hbm.at[j], chol.at[j], chol_sem.at[j]).wait()
        for w in range(n):
            wide[pl.ds(w, BS, stride=n), :] = received[j, w].astype(jnp.float32)
        for i in range(BS):
            flat[:, i * BS : (i + 1) * BS] = wide[i * n : (i + 1) * n, :].astype(jnp.bfloat16)

        bias = jnp.zeros((n, vectors), jnp.float32)
        for c in range(area // CHUNK):
            bias = bias + lax.dot_general(
                flat[:, c * CHUNK : (c + 1) * CHUNK],
                chol[j, :, c * CHUNK : (c + 1) * CHUNK],
                (((1,), (1,)), ((), ())),
                preferred_element_type=jnp.float32,
            )
        bias_tiles[j] = bias
        shifted = (field_tiles[j] + bias).astype(jnp.bfloat16)
        for c in range(area // CHUNK):
            piece = jnp.dot(
                shifted,
                chol[j, :, c * CHUNK : (c + 1) * CHUNK],
                preferred_element_type=jnp.float32,
            )
            for i in range(CHUNK // BS):
                base = (c * (CHUNK // BS) + i) * n
                wide[base : base + n, :] = piece[:, i * BS : (i + 1) * BS]
        for w in range(n):
            back[j, w] = wide[pl.ds(w, BS, stride=n), :].astype(jnp.bfloat16)

        send_back(j, lax.rem(me + half, n))

        def pair(i, c):
            send_back(j, lax.rem(me + half + i, n))
            send_back(j, lax.rem(me + i, n))
            return c

        lax.fori_loop(1, half, pair, 0)
        pltpu.make_async_copy(
            back.at[j, me], returned.at[me * tiles + j], own_sem.at[j]
        ).start()
        return carry

    lax.fori_loop(0, tiles, process, 0)

    for j in range(tiles):
        bias_out[:, j * vectors : (j + 1) * vectors] = bias_tiles[j]

    others = pl.ds(0, (n - 1) * tiles)
    pltpu.make_async_copy(green.at[others], green.at[others], green_send).wait()
    pltpu.make_async_copy(green.at[others], green.at[others], back_send).wait()
    for j in range(tiles):
        pltpu.make_async_copy(
            back.at[j, me], returned.at[me * tiles + j], own_sem.at[j]
        ).wait()
    pltpu.make_async_copy(returned.at[others], returned.at[others], back_recv).wait()


def build_kernel(group, tile_block, walkers, left_factor, green, rows):
    count = green.shape[0]
    side = rows.shape[0]
    for r in range(side):
        rows[r] = walkers[0, :, r * BS : (r + 1) * BS].T

    def step(s, carry):
        for u in range(group):
            t = s * group + u
            block = tile_block[t]
            row = lax.div(block, side)
            col = block - row * side
            cols = left_factor[0, :, pl.ds(pl.multiple_of(col * BS, BS), BS)]
            green[t] = jnp.dot(rows[row], cols, preferred_element_type=jnp.float32).astype(
                jnp.bfloat16
            )
        return carry

    lax.fori_loop(0, count // group, step, 0)


def propagate_kernel(group, tile_block, parts, walkers, out, term, acc, total):
    count = parts.shape[0]
    side = walkers.shape[2] // BS
    term[...] = walkers[0]
    total[...] = walkers[0].astype(jnp.float32)
    for order in range(1, 4):
        acc[...] = jnp.zeros_like(acc)

        def step(s, carry):
            found = []
            for u in range(group):
                t = s * group + u
                block = tile_block[t]
                row = lax.div(block, side)
                col = block - row * side
                piece = term[:, pl.ds(pl.multiple_of(col * BS, BS), BS)]
                product = lax.dot_general(
                    piece,
                    parts[t],
                    (((1,), (1,)), ((), ())),
                    preferred_element_type=jnp.float32,
                )
                found.append((row, product))
            for row, product in found:
                place = pl.ds(pl.multiple_of(row * BS, BS), BS)
                acc[:, place] = acc[:, place] + product
            return carry

        lax.fori_loop(0, count // group, step, 0)
        new = (acc[...] * (-step_root) / order).astype(jnp.bfloat16)
        if order < 3:
            term[...] = new
            total[...] = total[...] + new.astype(jnp.float32)
        else:
            out[0] = (total[...] + new.astype(jnp.float32)).astype(jnp.bfloat16)


def per_device(n, walkers, left_factor, chol_tiles, tile_block, fields):
    _, orbital_count, occupied = walkers.shape
    tiles, vectors, area = chol_tiles.shape
    all_tiles = n * tiles
    vmem = pl.BlockSpec(memory_space=pltpu.VMEM)
    smem = pl.BlockSpec(memory_space=pltpu.SMEM)
    anywhere = pl.BlockSpec(memory_space=pl.ANY)
    turned = walkers.transpose(0, 2, 1)
    green = pl.pallas_call(
        functools.partial(build_kernel, 4),
        out_shape=jax.ShapeDtypeStruct((all_tiles, BS, BS), jnp.bfloat16),
        in_specs=[smem, vmem, vmem],
        out_specs=vmem,
        scratch_shapes=[pltpu.VMEM((orbital_count // BS, BS, occupied), jnp.bfloat16)],
        compiler_params=pltpu.CompilerParams(vmem_limit_bytes=32 * 2**20),
        name="build",
    )(tile_block, turned, left_factor)
    force_bias, returned = pl.pallas_call(
        functools.partial(exchange_kernel, n),
        out_shape=(
            jax.ShapeDtypeStruct((n, tiles * vectors), jnp.float32),
            jax.ShapeDtypeStruct((all_tiles, BS, BS), jnp.bfloat16),
        ),
        in_specs=[vmem, vmem, anywhere],
        out_specs=(vmem, anywhere),
        scratch_shapes=[
            pltpu.VMEM((tiles, vectors, area), jnp.bfloat16),
            pltpu.VMEM((tiles, n, BS, BS), jnp.bfloat16),
            pltpu.VMEM((tiles, n, BS, BS), jnp.bfloat16),
            pltpu.VMEM((BS * n, BS), jnp.float32),
            pltpu.VMEM((n, area), jnp.bfloat16),
            pltpu.VMEM((tiles, n, vectors), jnp.float32),
            pltpu.VMEM((tiles, n, vectors), jnp.float32),
            pltpu.SemaphoreType.DMA((tiles,)),
            pltpu.SemaphoreType.DMA,
            pltpu.SemaphoreType.DMA((tiles,)),
            pltpu.SemaphoreType.DMA,
            pltpu.SemaphoreType.DMA,
            pltpu.SemaphoreType.DMA((tiles,)),
        ],
        compiler_params=pltpu.CompilerParams(
            collective_id=0, has_side_effects=True, vmem_limit_bytes=48 * 2**20
        ),
        name="exchange",
    )(green, fields, chol_tiles)
    new_walkers = pl.pallas_call(
        functools.partial(propagate_kernel, 8),
        out_shape=jax.ShapeDtypeStruct(turned.shape, jnp.bfloat16),
        in_specs=[smem, vmem, vmem],
        out_specs=vmem,
        scratch_shapes=[
            pltpu.VMEM((occupied, orbital_count), jnp.bfloat16),
            pltpu.VMEM((occupied, orbital_count), jnp.float32),
            pltpu.VMEM((occupied, orbital_count), jnp.float32),
        ],
        compiler_params=pltpu.CompilerParams(vmem_limit_bytes=48 * 2**20),
        name="propagate",
    )(tile_block, returned, turned)
    return (force_bias, new_walkers.transpose(0, 2, 1))


def solution(mesh):
    in_specs = (
        P(("parts", "chol"), None, None),
        P(("parts", "chol"), None, None),
        P("chol", None, None),
        P(),
        P("parts", "chol"),
    )
    out_specs = (P("parts", "chol"), P(("parts", "chol"), None, None))
    return jax.shard_map(
        functools.partial(per_device, mesh.shape["chol"]),
        mesh=mesh,
        in_specs=in_specs,
        out_specs=out_specs,
        check_vma=False,
    )
```

time: 254 us -> 120 us (0.47)
  the two profiles are of different devices: /device:TPU:13 before, /device:TPU:0 now
where the time goes in v1:
time: 120 us
  Pallas kernels  115 us (96%)
  local copies, waits for them, and re-layouts  4.02 us (3%)
    pallas_call x1, Pallas kernels, per_device(): pl.pallas_call(functools.partial(exchange_kernel, n), out_shape=(jax.Shap...  97.7 us
    pallas_call x1, Pallas kernels, per_device(): pl.pallas_call(functools.partial(propagate_kernel, 8), out_shape=jax.Shap...  12.5 us
    pallas_call x1, Pallas kernels, per_device(): pl.pallas_call(functools.partial(build_kernel, 4), out_shape=jax.ShapeDty...  5.22 us
    unnamed x13, local copies, waits for them, and re-layouts  4.02 us

profile of v1, /device:TPU:0, one launch (start us, length us, event | category | flops | bytes accessed | tf_op | source)
XLA Modules:
  0.0 120.1 jit_solution(16227472039785651761)
XLA Ops:
  0.6 0.0 copy-start
  0.6 1.4 %copy-done = bf16[1,2304,320]{1,2,0:T(8,128)(2,1)S(1)} copy-done((bf16[1,2304,320]{1,2,0:T(8,128)(2,1)S(1)}, bf16[1,2304,320]{1,2,0:T(8,128)(2,1)}, u32[]{:S(2)}) %copy-start) | copy-done | bytes 1474584
  2.0 0.0 copy-start.2
  2.0 1.4 %copy-done.2 = bf16[1,320,2304]{2,1,0:T(8,128)(2,1)S(1)} copy-done((bf16[1,320,2304]{2,1,0:T(8,128)(2,1)S(1)}, bf16[1,320,2304]{2,1,0:T(8,128)(2,1)}, u32[]{:S(2)}) %copy-start.2) | copy-done | bytes 1474584
  3.4 0.0 copy-start.4
  3.4 0.7 copy-done.4
  4.0 0.0 copy-start.3
  4.0 5.2 %build.1.green = bf16[64,128,128]{2,1,0:T(8,128)(2,1)S(1)} custom-call(s32[64]{0:T(128)S(1)} %copy-done.4, bf16[1,320,2304]{2,1,0:T(8,128)(2,1)S(1)} %bitcast.2, bf16[1,320,2304]{2,1,0:T(8,128)(2,1)S(1)} %copy-done.2), custom_call_target="tpu_custom_call" | custom-call | tf_op jit(solution)/shard_map/build/pallas_call | solution.py:224
  9.3 0.0 copy-done.3
  9.3 0.0 copy-start.1
  9.3 0.0 copy-start.5
  9.3 97.7 %exchange.1 = (f32[16,192]{1,0:T(8,128)S(1)}, bf16[64,128,128]{2,1,0:T(8,128)(2,1)S(1)}) custom-call(bf16[64,128,128]{2,1,0:T(8,128)(2,1)S(1)} %build.1.green, f32[16,192]{1,0:T(8,128)S(1)} %copy-done.3, bf16[4,48,16384]{2,1,0:T(8,128)(2,1)} %chol_hbm.1), custom_call_target="tpu_custom_call" | custom-call | tf_op jit(solution)/shard_map/exchange/pallas_call | solution.py:233
  107.0 0.0 copy-done.1
  107.0 0.0 copy-done.5
  107.0 12.5 %propagate.1 = bf16[1,320,2304]{2,1,0:T(8,128)(2,1)} custom-call(s32[64]{0:T(128)S(1)} %copy-done.5, bf16[64,128,128]{2,1,0:T(8,128)(2,1)S(1)} %get-tuple-element.5.parts, bf16[1,320,2304]{2,1,0:T(8,128)(2,1)S(1)} %bitcast.3), custom_call_target="tpu_custom_call" | custom-call | tf_op jit(solution)/shard_map/propagate/pallas_call | solution.py:261
  119.5 0.6 copy.8
Async XLA Ops:
  0.6 1.4 %copy-start = (bf16[1,2304,320]{1,2,0:T(8,128)(2,1)S(1)}, bf16[1,2304,320]{1,2,0:T(8,128)(2,1)}, u32[]{:S(2)}) copy-start(bf16[1,2304,320]{1,2,0:T(8,128)(2,1)} %param.5) | copy-start | bytes 4423684
  2.0 1.4 %copy-start.2 = (bf16[1,320,2304]{2,1,0:T(8,128)(2,1)S(1)}, bf16[1,320,2304]{2,1,0:T(8,128)(2,1)}, u32[]{:S(2)}) copy-start(bf16[1,320,2304]{2,1,0:T(8,128)(2,1)} %left_factor.1) | copy-start | bytes 4423684
  3.4 0.7 copy-start.4
  4.0 5.2 %copy-start.3 = (f32[16,192]{1,0:T(8,128)S(1)}, f32[16,192]{1,0:T(8,128)}, u32[]{:S(2)}) copy-start(f32[16,192]{1,0:T(8,128)} %fields.1) | copy-start | bytes 36868
  9.3 97.7 %copy-start.1 = (bf16[1,2304,320]{1,2,0:T(8,128)(2,1)S(1)}, bf16[1,2304,320]{1,2,0:T(8,128)(2,1)}, u32[]{:S(2)}) copy-start(bf16[1,2304,320]{1,2,0:T(8,128)(2,1)} %param.5) | copy-start | bytes 4423684
  9.3 97.7 %copy-start.5 = (s32[64]{0:T(128)S(1)}, s32[64]{0:T(128)}, u32[]{:S(2)}) copy-start(s32[64]{0:T(128)} %tile_block.3) | copy-start | bytes 772

commit v2 on v1

--- a/solution.py
+++ b/solution.py
@@ -16,18 +16,26 @@
 
 def exchange_kernel(
     n,
-    green,
+    tile_block,
+    turned_hbm,
+    factor_hbm,
     fields,
     chol_hbm,
     bias_out,
     returned,
     chol,
+    turned,
+    factor,
+    rows,
+    cols,
+    green,
     received,
     back,
     wide,
     flat,
     field_tiles,
     bias_tiles,
+    in_sem,
     chol_sem,
     green_send,
     green_recv,
@@ -40,6 +48,11 @@
     tiles, vectors, area = chol.shape
     half = n // 2
 
+    side = rows.shape[0]
+    turned_copy = pltpu.make_async_copy(turned_hbm.at[0], turned, in_sem.at[0])
+    factor_copy = pltpu.make_async_copy(factor_hbm.at[0], factor, in_sem.at[1])
+    turned_copy.start()
+    factor_copy.start()
     chol_copies = [
         pltpu.make_async_copy(chol_hbm.at[j], chol.at[j], chol_sem.at[j]) for j in range(tiles)
     ]
@@ -59,8 +72,24 @@
     for j in range(tiles):
         field_tiles[j] = fields[:, j * vectors : (j + 1) * vectors]
 
+    turned_copy.wait()
+    for r in range(side):
+        rows[r] = turned[:, r * BS : (r + 1) * BS].T
+    factor_copy.wait()
+    for r in range(side):
+        cols[r] = factor[:, r * BS : (r + 1) * BS]
+
+    def build(t):
+        block = tile_block[t]
+        row = lax.div(block, side)
+        col = block - row * side
+        return jnp.dot(rows[row], cols[col], preferred_element_type=jnp.float32).astype(
+            jnp.bfloat16
+        )
+
     def send_green(j, owner):
         t = owner * tiles + j
+        green[t] = build(t)
         pltpu.make_async_remote_copy(
             src_ref=green.at[t],
             dst_ref=received.at[j, me],
@@ -70,8 +99,6 @@
             device_id_type=MESH,
         ).start()
 
-    for j in range(tiles):
-        received[j, me] = green[me * tiles + j]
     pl.semaphore_wait(barrier, n - 1)
 
     def send_tile(j, carry):
@@ -85,6 +112,8 @@
         return lax.fori_loop(1, half, pair, carry)
 
     lax.fori_loop(0, tiles, send_tile, 0)
+    for j in range(tiles):
+        received[j, me] = build(me * tiles + j)
 
     def send_back(j, walker):
         pltpu.make_async_remote_copy(
@@ -155,30 +184,28 @@
     pltpu.make_async_copy(returned.at[others], returned.at[others], back_recv).wait()
 
 
-def build_kernel(group, tile_block, walkers, left_factor, green, rows):
-    count = green.shape[0]
-    side = rows.shape[0]
-    for r in range(side):
-        rows[r] = walkers[0, :, r * BS : (r + 1) * BS].T
-
-    def step(s, carry):
+def propagate_kernel(
+    group, tile_block, parts, walkers, bias, out, bias_out, paired, term, acc, total, bias_sem
+):
+    bias_copy = pltpu.make_async_copy(bias, bias_out, bias_sem)
+    bias_copy.start()
+    pairs = paired.shape[0]
+    side = walkers.shape[2] // BS
+    zero = jnp.zeros((BS, BS), jnp.bfloat16)
+
+    def place_of(index):
+        return pl.ds(pl.multiple_of(index * BS, BS), BS)
+
+    def pair_up(s, carry):
         for u in range(group):
-            t = s * group + u
-            block = tile_block[t]
-            row = lax.div(block, side)
-            col = block - row * side
-            cols = left_factor[0, :, pl.ds(pl.multiple_of(col * BS, BS), BS)]
-            green[t] = jnp.dot(rows[row], cols, preferred_element_type=jnp.float32).astype(
-                jnp.bfloat16
-            )
+            q = s * group + u
+            paired[q, :BS, :BS] = parts[2 * q]
+            paired[q, :BS, BS:] = zero
+            paired[q, BS:, :BS] = zero
+            paired[q, BS:, BS:] = parts[2 * q + 1]
         return carry
 
-    lax.fori_loop(0, count // group, step, 0)
-
-
-def propagate_kernel(group, tile_block, parts, walkers, out, term, acc, total):
-    count = parts.shape[0]
-    side = walkers.shape[2] // BS
+    lax.fori_loop(0, pairs // group, pair_up, 0)
     term[...] = walkers[0]
     total[...] = walkers[0].astype(jnp.float32)
     for order in range(1, 4):
@@ -187,30 +214,33 @@
         def step(s, carry):
             found = []
             for u in range(group):
-                t = s * group + u
-                block = tile_block[t]
-                row = lax.div(block, side)
-                col = block - row * side
-                piece = term[:, pl.ds(pl.multiple_of(col * BS, BS), BS)]
+                q = s * group + u
+                places, pieces = [], []
+                for t in (2 * q, 2 * q + 1):
+                    block = tile_block[t]
+                    row = lax.div(block, side)
+                    places.append(place_of(row))
+                    pieces.append(term[:, place_of(block - row * side)])
                 product = lax.dot_general(
-                    piece,
-                    parts[t],
+                    jnp.concatenate(pieces, axis=1),
+                    paired[q],
                     (((1,), (1,)), ((), ())),
                     preferred_element_type=jnp.float32,
                 )
-                found.append((row, product))
-            for row, product in found:
-                place = pl.ds(pl.multiple_of(row * BS, BS), BS)
-                acc[:, place] = acc[:, place] + product
+                found.append((places, product))
+            for places, product in found:
+                acc[:, places[0]] = acc[:, places[0]] + product[:, :BS]
+                acc[:, places[1]] = acc[:, places[1]] + product[:, BS:]
             return carry
 
-        lax.fori_loop(0, count // group, step, 0)
+        lax.fori_loop(0, pairs // group, step, 0)
         new = (acc[...] * (-step_root) / order).astype(jnp.bfloat16)
         if order < 3:
             term[...] = new
             total[...] = total[...] + new.astype(jnp.float32)
         else:
             out[0] = (total[...] + new.astype(jnp.float32)).astype(jnp.bfloat16)
+    bias_copy.wait()
 
 
 def per_device(n, walkers, left_factor, chol_tiles, tile_block, fields):
@@ -221,31 +251,28 @@
     smem = pl.BlockSpec(memory_space=pltpu.SMEM)
     anywhere = pl.BlockSpec(memory_space=pl.ANY)
     turned = walkers.transpose(0, 2, 1)
-    green = pl.pallas_call(
-        functools.partial(build_kernel, 4),
-        out_shape=jax.ShapeDtypeStruct((all_tiles, BS, BS), jnp.bfloat16),
-        in_specs=[smem, vmem, vmem],
-        out_specs=vmem,
-        scratch_shapes=[pltpu.VMEM((orbital_count // BS, BS, occupied), jnp.bfloat16)],
-        compiler_params=pltpu.CompilerParams(vmem_limit_bytes=32 * 2**20),
-        name="build",
-    )(tile_block, turned, left_factor)
     force_bias, returned = pl.pallas_call(
         functools.partial(exchange_kernel, n),
         out_shape=(
             jax.ShapeDtypeStruct((n, tiles * vectors), jnp.float32),
             jax.ShapeDtypeStruct((all_tiles, BS, BS), jnp.bfloat16),
         ),
-        in_specs=[vmem, vmem, anywhere],
+        in_specs=[smem, anywhere, anywhere, vmem, anywhere],
         out_specs=(vmem, anywhere),
         scratch_shapes=[
             pltpu.VMEM((tiles, vectors, area), jnp.bfloat16),
+            pltpu.VMEM((occupied, orbital_count), jnp.bfloat16),
+            pltpu.VMEM((occupied, orbital_count), jnp.bfloat16),
+            pltpu.VMEM((orbital_count // BS, BS, occupied), jnp.bfloat16),
+            pltpu.VMEM((orbital_count // BS, occupied, BS), jnp.bfloat16),
+            pltpu.VMEM((all_tiles, BS, BS), jnp.bfloat16),
             pltpu.VMEM((tiles, n, BS, BS), jnp.bfloat16),
             pltpu.VMEM((tiles, n, BS, BS), jnp.bfloat16),
             pltpu.VMEM((BS * n, BS), jnp.float32),
             pltpu.VMEM((n, area), jnp.bfloat16),
             pltpu.VMEM((tiles, n, vectors), jnp.float32),
             pltpu.VMEM((tiles, n, vectors), jnp.float32),
+            pltpu.SemaphoreType.DMA((2,)),
             pltpu.SemaphoreType.DMA((tiles,)),
             pltpu.SemaphoreType.DMA,
             pltpu.SemaphoreType.DMA((tiles,)),
@@ -257,20 +284,25 @@
             collective_id=0, has_side_effects=True, vmem_limit_bytes=48 * 2**20
         ),
         name="exchange",
-    )(green, fields, chol_tiles)
-    new_walkers = pl.pallas_call(
-        functools.partial(propagate_kernel, 8),
-        out_shape=jax.ShapeDtypeStruct(turned.shape, jnp.bfloat16),
-        in_specs=[smem, vmem, vmem],
-        out_specs=vmem,
+    )(tile_block, turned, left_factor, fields, chol_tiles)
+    new_walkers, force_bias = pl.pallas_call(
+        functools.partial(propagate_kernel, 4),
+        out_shape=(
+            jax.ShapeDtypeStruct(turned.shape, jnp.bfloat16),
+            jax.ShapeDtypeStruct(force_bias.shape, jnp.float32),
+        ),
+        in_specs=[smem, vmem, vmem, vmem],
+        out_specs=(vmem, anywhere),
         scratch_shapes=[
+            pltpu.VMEM((all_tiles // 2, 2 * BS, 2 * BS), jnp.bfloat16),
             pltpu.VMEM((occupied, orbital_count), jnp.bfloat16),
             pltpu.VMEM((occupied, orbital_count), jnp.float32),
             pltpu.VMEM((occupied, orbital_count), jnp.float32),
+            pltpu.SemaphoreType.DMA,
         ],
         compiler_params=pltpu.CompilerParams(vmem_limit_bytes=48 * 2**20),
         name="propagate",
-    )(tile_block, returned, turned)
+    )(tile_block, returned, turned, force_bias)
     return (force_bias, new_walkers.transpose(0, 2, 1))
 
 

time: 120 us -> 119 us (level)
    pallas_call x2 -> x1, Pallas kernels: 17.7 us -> 14.9 us  [per_device(): pl.pallas_call(functools.partial(propagate_kernel, 4), out_shape=(jax.Sha...]
    pallas_call x1, Pallas kernels: 97.7 us -> 99 us  [per_device(): pl.pallas_call(functools.partial(exchange_kernel, n), out_shape=(jax.Shap...]
    unnamed x13 -> x8, local copies, waits for them, and re-layouts: 4.02 us -> 4.11 us
where the time goes in v2:
time: 119 us
  Pallas kernels  114 us (96%)
  local copies, waits for them, and re-layouts  4.11 us (3%)
    pallas_call x1, Pallas kernels, per_device(): pl.pallas_call(functools.partial(exchange_kernel, n), out_shape=(jax.Shap...  99 us
    pallas_call x1, Pallas kernels, per_device(): pl.pallas_call(functools.partial(propagate_kernel, 4), out_shape=(jax.Sha...  14.9 us
    unnamed x8, local copies, waits for them, and re-layouts  4.11 us

profile of v2, /device:TPU:0, one launch (start us, length us, event | category | flops | bytes accessed | tf_op | source)
XLA Modules:
  0.0 118.7 jit_solution(6968441458404980119)
XLA Ops:
  0.6 0.0 copy-start
  0.6 1.4 %copy-done = bf16[1,2304,320]{1,2,0:T(8,128)(2,1)S(1)} copy-done((bf16[1,2304,320]{1,2,0:T(8,128)(2,1)S(1)}, bf16[1,2304,320]{1,2,0:T(8,128)(2,1)}, u32[]{:S(2)}) %copy-start) | copy-done | bytes 1474584
  2.0 0.0 copy-start.1
  2.0 1.4 %copy-done.1 = bf16[1,320,2304]{2,1,0:T(8,128)(2,1)S(1)} copy-done((bf16[1,320,2304]{2,1,0:T(8,128)(2,1)S(1)}, bf16[1,320,2304]{2,1,0:T(8,128)(2,1)}, u32[]{:S(2)}) %copy-start.1) | copy-done | bytes 1474584
  3.4 0.0 copy-start.2
  3.4 0.7 copy-done.2
  4.1 0.0 copy-start.3
  4.1 0.7 copy-done.3
  4.8 99.0 %exchange.1 = (f32[16,192]{1,0:T(8,128)S(1)}, bf16[64,128,128]{2,1,0:T(8,128)(2,1)S(1)}) custom-call(s32[64]{0:T(128)S(1)} %copy-done.3, bf16[1,320,2304]{2,1,0:T(8,128)(2,1)S(1)} %bitcast.2, bf16[1,320,2304]{2,1,0:T(8,128)(2,1)S(1)} %copy-done.1, f32[16,192]{1,0:T(8,128)S(1)} %copy-done.2, bf16[4,48,16384]{2,1,0:T(8,128)(2,1)} %chol_hbm.1), custom_call_target="tpu_custom_call" | custom-call | tf_op jit(solution)/shard_map/exchange/pallas_call | solution.py:254
  103.8 14.9 %propagate.1 = (bf16[1,320,2304]{2,1,0:T(8,128)(2,1)}, f32[16,192]{1,0:T(8,128)}) custom-call(s32[64]{0:T(128)S(1)} %copy-done.3, bf16[64,128,128]{2,1,0:T(8,128)(2,1)S(1)} %get-tuple-element.6.parts, bf16[1,320,2304]{2,1,0:T(8,128)(2,1)S(1)} %bitcast.3, f32[16,192]{1,0:T(8,128)S(1)} %get-tuple-element.7.bias), custom_call_target="tpu_custom_call" | custom-call | tf_op jit(solution)/shard_map/propagate/pallas_call | solution.py:288
Async XLA Ops:
  0.6 1.4 %copy-start = (bf16[1,2304,320]{1,2,0:T(8,128)(2,1)S(1)}, bf16[1,2304,320]{1,2,0:T(8,128)(2,1)}, u32[]{:S(2)}) copy-start(bf16[1,2304,320]{1,2,0:T(8,128)(2,1)} %param.5) | copy-start | bytes 4423684
  2.0 1.4 %copy-start.1 = (bf16[1,320,2304]{2,1,0:T(8,128)(2,1)S(1)}, bf16[1,320,2304]{2,1,0:T(8,128)(2,1)}, u32[]{:S(2)}) copy-start(bf16[1,320,2304]{2,1,0:T(8,128)(2,1)} %factor_hbm.1) | copy-start | bytes 4423684
  3.4 0.7 copy-start.2
  4.1 0.7 copy-start.3

commit v3 on v2

--- a/solution.py
+++ b/solution.py
@@ -24,8 +24,7 @@
     bias_out,
     returned,
     chol,
-    turned,
-    factor,
+    fields_here,
     rows,
     cols,
     green,
@@ -49,10 +48,12 @@
     half = n // 2
 
     side = rows.shape[0]
-    turned_copy = pltpu.make_async_copy(turned_hbm.at[0], turned, in_sem.at[0])
-    factor_copy = pltpu.make_async_copy(factor_hbm.at[0], factor, in_sem.at[1])
-    turned_copy.start()
-    factor_copy.start()
+    for r in range(side):
+        place = pl.ds(r * BS, BS)
+        pltpu.make_async_copy(turned_hbm.at[0, :, place], rows.at[r], in_sem.at[0]).start()
+        pltpu.make_async_copy(factor_hbm.at[0, :, place], cols.at[r], in_sem.at[1]).start()
+    fields_copy = pltpu.make_async_copy(fields, fields_here, in_sem.at[2])
+    fields_copy.start()
     chol_copies = [
         pltpu.make_async_copy(chol_hbm.at[j], chol.at[j], chol_sem.at[j]) for j in range(tiles)
     ]
@@ -69,23 +70,19 @@
 
     lax.fori_loop(1, n, greet, 0)
 
-    for j in range(tiles):
-        field_tiles[j] = fields[:, j * vectors : (j + 1) * vectors]
-
-    turned_copy.wait()
-    for r in range(side):
-        rows[r] = turned[:, r * BS : (r + 1) * BS].T
-    factor_copy.wait()
-    for r in range(side):
-        cols[r] = factor[:, r * BS : (r + 1) * BS]
+    pltpu.make_async_copy(rows, rows, in_sem.at[0]).wait()
+    pltpu.make_async_copy(cols, cols, in_sem.at[1]).wait()
 
     def build(t):
         block = tile_block[t]
         row = lax.div(block, side)
         col = block - row * side
-        return jnp.dot(rows[row], cols[col], preferred_element_type=jnp.float32).astype(
-            jnp.bfloat16
-        )
+        return lax.dot_general(
+            rows[row],
+            cols[col],
+            (((0,), (0,)), ((), ())),
+            preferred_element_type=jnp.float32,
+        ).astype(jnp.bfloat16)
 
     def send_green(j, owner):
         t = owner * tiles + j
@@ -114,6 +111,9 @@
     lax.fori_loop(0, tiles, send_tile, 0)
     for j in range(tiles):
         received[j, me] = build(me * tiles + j)
+    fields_copy.wait()
+    for j in range(tiles):
+        field_tiles[j] = fields_here[:, j * vectors : (j + 1) * vectors]
 
     def send_back(j, walker):
         pltpu.make_async_remote_copy(
@@ -185,61 +185,49 @@
 
 
 def propagate_kernel(
-    group, tile_block, parts, walkers, bias, out, bias_out, paired, term, acc, total, bias_sem
+    group, tile_block, parts, walkers, bias, out, bias_out, term, acc, total, bias_sem, out_sem
 ):
     bias_copy = pltpu.make_async_copy(bias, bias_out, bias_sem)
     bias_copy.start()
-    pairs = paired.shape[0]
-    side = walkers.shape[2] // BS
-    zero = jnp.zeros((BS, BS), jnp.bfloat16)
-
-    def place_of(index):
-        return pl.ds(pl.multiple_of(index * BS, BS), BS)
-
-    def pair_up(s, carry):
-        for u in range(group):
-            q = s * group + u
-            paired[q, :BS, :BS] = parts[2 * q]
-            paired[q, :BS, BS:] = zero
-            paired[q, BS:, :BS] = zero
-            paired[q, BS:, BS:] = parts[2 * q + 1]
-        return carry
-
-    lax.fori_loop(0, pairs // group, pair_up, 0)
-    term[...] = walkers[0]
-    total[...] = walkers[0].astype(jnp.float32)
+    count = parts.shape[0]
+    side = term.shape[0]
+    for r in range(side):
+        term[r] = walkers[0, :, r * BS : (r + 1) * BS]
     for order in range(1, 4):
-        acc[...] = jnp.zeros_like(acc)
+        for r in range(side):
+            acc[r] = jnp.zeros(acc.shape[1:], jnp.float32)
 
         def step(s, carry):
-            found = []
             for u in range(group):
-                q = s * group + u
-                places, pieces = [], []
-                for t in (2 * q, 2 * q + 1):
-                    block = tile_block[t]
-                    row = lax.div(block, side)
-                    places.append(place_of(row))
-                    pieces.append(term[:, place_of(block - row * side)])
-                product = lax.dot_general(
-                    jnp.concatenate(pieces, axis=1),
-                    paired[q],
+                t = s * group + u
+                block = tile_block[t]
+                row = lax.div(block, side)
+                col = block - row * side
+                acc[row] = acc[row] + lax.dot_general(
+                    term[col],
+                    parts[t],
                     (((1,), (1,)), ((), ())),
                     preferred_element_type=jnp.float32,
                 )
-                found.append((places, product))
-            for places, product in found:
-                acc[:, places[0]] = acc[:, places[0]] + product[:, :BS]
-                acc[:, places[1]] = acc[:, places[1]] + product[:, BS:]
             return carry
 
-        lax.fori_loop(0, pairs // group, step, 0)
-        new = (acc[...] * (-step_root) / order).astype(jnp.bfloat16)
-        if order < 3:
-            term[...] = new
-            total[...] = total[...] + new.astype(jnp.float32)
-        else:
-            out[0] = (total[...] + new.astype(jnp.float32)).astype(jnp.bfloat16)
+        lax.fori_loop(0, count // group, step, 0)
+        for r in range(side):
+            new = (acc[r] * (-step_root) / order).astype(jnp.bfloat16)
+            if order == 1:
+                before = walkers[0, :, r * BS : (r + 1) * BS].astype(jnp.float32)
+            else:
+                before = total[r]
+            after = before + new.astype(jnp.float32)
+            if order < 3:
+                term[r] = new
+                total[r] = after
+            else:
+                term[r] = after.astype(jnp.bfloat16)
+                pltpu.make_async_copy(
+                    term.at[r], out.at[0, :, pl.ds(r * BS, BS)], out_sem
+                ).start()
+    pltpu.make_async_copy(term, term, out_sem).wait()
     bias_copy.wait()
 
 
@@ -247,8 +235,10 @@
     _, orbital_count, occupied = walkers.shape
     tiles, vectors, area = chol_tiles.shape
     all_tiles = n * tiles
+    side = orbital_count // BS
     vmem = pl.BlockSpec(memory_space=pltpu.VMEM)
     smem = pl.BlockSpec(memory_space=pltpu.SMEM)
+    hbm = pl.BlockSpec(memory_space=pltpu.HBM)
     anywhere = pl.BlockSpec(memory_space=pl.ANY)
     turned = walkers.transpose(0, 2, 1)
     force_bias, returned = pl.pallas_call(
@@ -257,14 +247,13 @@
             jax.ShapeDtypeStruct((n, tiles * vectors), jnp.float32),
             jax.ShapeDtypeStruct((all_tiles, BS, BS), jnp.bfloat16),
         ),
-        in_specs=[smem, anywhere, anywhere, vmem, anywhere],
+        in_specs=[smem, hbm, hbm, hbm, hbm],
         out_specs=(vmem, anywhere),
         scratch_shapes=[
             pltpu.VMEM((tiles, vectors, area), jnp.bfloat16),
-            pltpu.VMEM((occupied, orbital_count), jnp.bfloat16),
-            pltpu.VMEM((occupied, orbital_count), jnp.bfloat16),
-            pltpu.VMEM((orbital_count // BS, BS, occupied), jnp.bfloat16),
-            pltpu.VMEM((orbital_count // BS, occupied, BS), jnp.bfloat16),
+            pltpu.VMEM((n, tiles * vectors), jnp.float32),
+            pltpu.VMEM((side, occupied, BS), jnp.bfloat16),
+            pltpu.VMEM((side, occupied, BS), jnp.bfloat16),
             pltpu.VMEM((all_tiles, BS, BS), jnp.bfloat16),
             pltpu.VMEM((tiles, n, BS, BS), jnp.bfloat16),
             pltpu.VMEM((tiles, n, BS, BS), jnp.bfloat16),
@@ -272,7 +261,7 @@
             pltpu.VMEM((n, area), jnp.bfloat16),
             pltpu.VMEM((tiles, n, vectors), jnp.float32),
             pltpu.VMEM((tiles, n, vectors), jnp.float32),
-            pltpu.SemaphoreType.DMA((2,)),
+            pltpu.SemaphoreType.DMA((3,)),
             pltpu.SemaphoreType.DMA((tiles,)),
             pltpu.SemaphoreType.DMA,
             pltpu.SemaphoreType.DMA((tiles,)),
@@ -286,18 +275,18 @@
         name="exchange",
     )(tile_block, turned, left_factor, fields, chol_tiles)
     new_walkers, force_bias = pl.pallas_call(
-        functools.partial(propagate_kernel, 4),
+        functools.partial(propagate_kernel, 16),
         out_shape=(
             jax.ShapeDtypeStruct(turned.shape, jnp.bfloat16),
             jax.ShapeDtypeStruct(force_bias.shape, jnp.float32),
         ),
         in_specs=[smem, vmem, vmem, vmem],
-        out_specs=(vmem, anywhere),
+        out_specs=(hbm, hbm),
         scratch_shapes=[
-            pltpu.VMEM((all_tiles // 2, 2 * BS, 2 * BS), jnp.bfloat16),
-            pltpu.VMEM((occupied, orbital_count), jnp.bfloat16),
-            pltpu.VMEM((occupied, orbital_count), jnp.float32),
-            pltpu.VMEM((occupied, orbital_count), jnp.float32),
+            pltpu.VMEM((side, occupied, BS), jnp.bfloat16),
+            pltpu.VMEM((side, occupied, BS), jnp.float32),
+            pltpu.VMEM((side, occupied, BS), jnp.float32),
+            pltpu.SemaphoreType.DMA,
             pltpu.SemaphoreType.DMA,
         ],
         compiler_params=pltpu.CompilerParams(vmem_limit_bytes=48 * 2**20),

time: 119 us -> 114 us (0.958)
  Pallas kernels: 114 us -> 109 us
    pallas_call x1, Pallas kernels: 14.9 us -> 9.74 us  [per_device(): pl.pallas_call(functools.partial(propagate_kernel, 16), out_shape=(jax.Sh...]
where the time goes in v3:
time: 114 us; the launch traced here: 113 us
  Pallas kernels  109 us (96%)
  local copies, waits for them, and re-layouts  4.11 us (4%)
    pallas_call x1, Pallas kernels, per_device(): pl.pallas_call(functools.partial(exchange_kernel, n), out_shape=(jax.Shap...  99 us
    pallas_call x1, Pallas kernels, per_device(): pl.pallas_call(functools.partial(propagate_kernel, 16), out_shape=(jax.Sh...  9.74 us
    unnamed x8, local copies, waits for them, and re-layouts  4.11 us

profile of v3, /device:TPU:0, one launch (start us, length us, event | category | flops | bytes accessed | tf_op | source)
XLA Modules:
  0.0 113.5 jit_solution(11201660216065914366)
XLA Ops:
  0.6 0.0 copy-start
  0.6 1.4 %copy-done = bf16[1,2304,320]{1,2,0:T(8,128)(2,1)S(1)} copy-done((bf16[1,2304,320]{1,2,0:T(8,128)(2,1)S(1)}, bf16[1,2304,320]{1,2,0:T(8,128)(2,1)}, u32[]{:S(2)}) %copy-start) | copy-done | bytes 1474584
  2.0 0.0 copy-start.1
  2.0 1.4 %copy-done.1 = bf16[1,320,2304]{2,1,0:T(8,128)(2,1)S(1)} copy-done((bf16[1,320,2304]{2,1,0:T(8,128)(2,1)S(1)}, bf16[1,320,2304]{2,1,0:T(8,128)(2,1)}, u32[]{:S(2)}) %copy-start.1) | copy-done | bytes 1474584
  3.4 0.0 copy-start.2
  3.4 0.7 copy-done.2
  4.1 0.0 copy-start.3
  4.1 0.7 copy-done.3
  4.8 99.0 %exchange.1 = (f32[16,192]{1,0:T(8,128)S(1)}, bf16[64,128,128]{2,1,0:T(8,128)(2,1)S(1)}) custom-call(s32[64]{0:T(128)S(1)} %copy-done.3, bf16[1,320,2304]{2,1,0:T(8,128)(2,1)S(1)} %bitcast.2, bf16[1,320,2304]{2,1,0:T(8,128)(2,1)S(1)} %copy-done.1, f32[16,192]{1,0:T(8,128)S(1)} %copy-done.2, bf16[4,48,16384]{2,1,0:T(8,128)(2,1)} %chol_hbm.1), custom_call_target="tpu_custom_call" | custom-call | tf_op jit(solution)/shard_map/exchange/pallas_call | solution.py:244
  103.7 9.7 %propagate.1 = (bf16[1,320,2304]{2,1,0:T(8,128)(2,1)}, f32[16,192]{1,0:T(8,128)}) custom-call(s32[64]{0:T(128)S(1)} %copy-done.3, bf16[64,128,128]{2,1,0:T(8,128)(2,1)S(1)} %get-tuple-element.6.parts, bf16[1,320,2304]{2,1,0:T(8,128)(2,1)S(1)} %bitcast.3, f32[16,192]{1,0:T(8,128)S(1)} %get-tuple-element.7.bias), custom_call_target="tpu_custom_call" | custom-call | tf_op jit(solution)/shard_map/propagate/pallas_call | solution.py:277
Async XLA Ops:
  0.6 1.4 %copy-start = (bf16[1,2304,320]{1,2,0:T(8,128)(2,1)S(1)}, bf16[1,2304,320]{1,2,0:T(8,128)(2,1)}, u32[]{:S(2)}) copy-start(bf16[1,2304,320]{1,2,0:T(8,128)(2,1)} %param.5) | copy-start | bytes 4423684
  2.0 1.4 %copy-start.1 = (bf16[1,320,2304]{2,1,0:T(8,128)(2,1)S(1)}, bf16[1,320,2304]{2,1,0:T(8,128)(2,1)}, u32[]{:S(2)}) copy-start(bf16[1,320,2304]{2,1,0:T(8,128)(2,1)} %factor_hbm.1) | copy-start | bytes 4423684
  3.4 0.7 copy-start.2
  4.1 0.7 copy-start.3

commit v4 on v3

--- a/solution.py
+++ b/solution.py
@@ -12,6 +12,7 @@
 
 step_root = 0.25
 CHUNK = 2048
+GROUP = 16
 
 
 def exchange_kernel(
@@ -34,6 +35,7 @@
     flat,
     field_tiles,
     bias_tiles,
+    bias_all,
     in_sem,
     chol_sem,
     green_send,
@@ -90,7 +92,7 @@
         pltpu.make_async_remote_copy(
             src_ref=green.at[t],
             dst_ref=received.at[j, me],
-            send_sem=green_send,
+            send_sem=green_send.at[j],
             recv_sem=green_recv.at[j],
             device_id=(part, owner),
             device_id_type=MESH,
@@ -108,7 +110,12 @@
 
         return lax.fori_loop(1, half, pair, carry)
 
-    lax.fori_loop(0, tiles, send_tile, 0)
+    def sent(j):
+        others = pl.ds(0, n - 1)
+        pltpu.make_async_copy(green.at[others], green.at[others], green_send.at[j]).wait()
+
+    ahead = min(2, tiles)
+    lax.fori_loop(0, ahead, send_tile, 0)
     for j in range(tiles):
         received[j, me] = build(me * tiles + j)
     fields_copy.wait()
@@ -126,6 +133,11 @@
         ).start()
 
     def process(j, carry):
+        @pl.when(j + ahead < tiles)
+        def _():
+            sent(j)
+            send_tile(j + ahead, 0)
+
         arrived = received.at[j, pl.ds(0, n - 1)]
         pltpu.make_async_copy(arrived, arrived, green_recv.at[j]).wait()
         pltpu.make_async_copy(chol_hbm.at[j], chol.at[j], chol_sem.at[j]).wait()
@@ -172,10 +184,14 @@
     lax.fori_loop(0, tiles, process, 0)
 
     for j in range(tiles):
-        bias_out[:, j * vectors : (j + 1) * vectors] = bias_tiles[j]
+        bias_all[:, j * vectors : (j + 1) * vectors] = bias_tiles[j]
+    bias_copy = pltpu.make_async_copy(bias_all, bias_out, in_sem.at[3])
+    bias_copy.start()
 
     others = pl.ds(0, (n - 1) * tiles)
-    pltpu.make_async_copy(green.at[others], green.at[others], green_send).wait()
+    bias_copy.wait()
+    for j in range(max(tiles - ahead, 0), tiles):
+        sent(j)
     pltpu.make_async_copy(green.at[others], green.at[others], back_send).wait()
     for j in range(tiles):
         pltpu.make_async_copy(
@@ -185,26 +201,55 @@
 
 
 def propagate_kernel(
-    group, tile_block, parts, walkers, bias, out, bias_out, term, acc, total, bias_sem, out_sem
+    group,
+    tile_block,
+    parts_hbm,
+    walkers_hbm,
+    bias,
+    out,
+    bias_out,
+    parts,
+    first,
+    term,
+    acc,
+    total,
+    bias_sem,
+    out_sem,
+    in_sem,
+    parts_sem,
 ):
+    count = parts.shape[0]
+    side = term.shape[0]
+
+    def group_copy(s):
+        place = pl.ds(s * group, group)
+        return pltpu.make_async_copy(parts_hbm.at[place], parts.at[place], parts_sem.at[s])
+
+    for r in range(side):
+        pltpu.make_async_copy(
+            walkers_hbm.at[0, :, pl.ds(r * BS, BS)], first.at[r], in_sem
+        ).start()
+    for s in range(count // group):
+        group_copy(s).start()
     bias_copy = pltpu.make_async_copy(bias, bias_out, bias_sem)
     bias_copy.start()
-    count = parts.shape[0]
-    side = term.shape[0]
-    for r in range(side):
-        term[r] = walkers[0, :, r * BS : (r + 1) * BS]
+    pltpu.make_async_copy(first, first, in_sem).wait()
     for order in range(1, 4):
         for r in range(side):
             acc[r] = jnp.zeros(acc.shape[1:], jnp.float32)
 
+        source = first if order == 1 else term
+
         def step(s, carry):
+            if order == 1:
+                group_copy(s).wait()
             for u in range(group):
                 t = s * group + u
                 block = tile_block[t]
                 row = lax.div(block, side)
                 col = block - row * side
                 acc[row] = acc[row] + lax.dot_general(
-                    term[col],
+                    source[col],
                     parts[t],
                     (((1,), (1,)), ((), ())),
                     preferred_element_type=jnp.float32,
@@ -215,7 +260,7 @@
         for r in range(side):
             new = (acc[r] * (-step_root) / order).astype(jnp.bfloat16)
             if order == 1:
-                before = walkers[0, :, r * BS : (r + 1) * BS].astype(jnp.float32)
+                before = first[r].astype(jnp.float32)
             else:
                 before = total[r]
             after = before + new.astype(jnp.float32)
@@ -236,10 +281,8 @@
     tiles, vectors, area = chol_tiles.shape
     all_tiles = n * tiles
     side = orbital_count // BS
-    vmem = pl.BlockSpec(memory_space=pltpu.VMEM)
     smem = pl.BlockSpec(memory_space=pltpu.SMEM)
     hbm = pl.BlockSpec(memory_space=pltpu.HBM)
-    anywhere = pl.BlockSpec(memory_space=pl.ANY)
     turned = walkers.transpose(0, 2, 1)
     force_bias, returned = pl.pallas_call(
         functools.partial(exchange_kernel, n),
@@ -248,7 +291,7 @@
             jax.ShapeDtypeStruct((all_tiles, BS, BS), jnp.bfloat16),
         ),
         in_specs=[smem, hbm, hbm, hbm, hbm],
-        out_specs=(vmem, anywhere),
+        out_specs=(hbm, hbm),
         scratch_shapes=[
             pltpu.VMEM((tiles, vectors, area), jnp.bfloat16),
             pltpu.VMEM((n, tiles * vectors), jnp.float32),
@@ -261,35 +304,40 @@
             pltpu.VMEM((n, area), jnp.bfloat16),
             pltpu.VMEM((tiles, n, vectors), jnp.float32),
             pltpu.VMEM((tiles, n, vectors), jnp.float32),
-            pltpu.SemaphoreType.DMA((3,)),
+            pltpu.VMEM((n, tiles * vectors), jnp.float32),
+            pltpu.SemaphoreType.DMA((4,)),
             pltpu.SemaphoreType.DMA((tiles,)),
-            pltpu.SemaphoreType.DMA,
+            pltpu.SemaphoreType.DMA((tiles,)),
             pltpu.SemaphoreType.DMA((tiles,)),
             pltpu.SemaphoreType.DMA,
             pltpu.SemaphoreType.DMA,
             pltpu.SemaphoreType.DMA((tiles,)),
         ],
         compiler_params=pltpu.CompilerParams(
-            collective_id=0, has_side_effects=True, vmem_limit_bytes=48 * 2**20
+            collective_id=0, has_side_effects=True, vmem_limit_bytes=60 * 2**20
         ),
         name="exchange",
     )(tile_block, turned, left_factor, fields, chol_tiles)
     new_walkers, force_bias = pl.pallas_call(
-        functools.partial(propagate_kernel, 16),
+        functools.partial(propagate_kernel, GROUP),
         out_shape=(
             jax.ShapeDtypeStruct(turned.shape, jnp.bfloat16),
             jax.ShapeDtypeStruct(force_bias.shape, jnp.float32),
         ),
-        in_specs=[smem, vmem, vmem, vmem],
+        in_specs=[smem, hbm, hbm, hbm],
         out_specs=(hbm, hbm),
         scratch_shapes=[
+            pltpu.VMEM((all_tiles, BS, BS), jnp.bfloat16),
+            pltpu.VMEM((side, occupied, BS), jnp.bfloat16),
             pltpu.VMEM((side, occupied, BS), jnp.bfloat16),
             pltpu.VMEM((side, occupied, BS), jnp.float32),
             pltpu.VMEM((side, occupied, BS), jnp.float32),
             pltpu.SemaphoreType.DMA,
             pltpu.SemaphoreType.DMA,
+            pltpu.SemaphoreType.DMA,
+            pltpu.SemaphoreType.DMA((all_tiles // GROUP,)),
         ],
-        compiler_params=pltpu.CompilerParams(vmem_limit_bytes=48 * 2**20),
+        compiler_params=pltpu.CompilerParams(vmem_limit_bytes=60 * 2**20),
         name="propagate",
     )(tile_block, returned, turned, force_bias)
     return (force_bias, new_walkers.transpose(0, 2, 1))

time: 114 us -> 112 us (0.982)
  local copies, waits for them, and re-layouts: 4.11 us -> 0 us
  Pallas kernels: 109 us -> 111 us
    unnamed x8 -> x0, local copies, waits for them, and re-layouts: 4.11 us -> none
    pallas_call x1, Pallas kernels: 9.74 us -> 11.5 us  [per_device(): pl.pallas_call(functools.partial(propagate_kernel, GROUP), out_shape=(jax...]
where the time goes in v4:
time: 112 us; the launch traced here: 111 us
  Pallas kernels  111 us (99%)
    pallas_call x1, Pallas kernels, per_device(): pl.pallas_call(functools.partial(exchange_kernel, n), out_shape=(jax.Shap...  99.3 us
    pallas_call x1, Pallas kernels, per_device(): pl.pallas_call(functools.partial(propagate_kernel, GROUP), out_shape=(jax...  11.5 us

profile of v4, /device:TPU:0, one launch (start us, length us, event | category | flops | bytes accessed | tf_op | source)
XLA Modules:
  0.0 111.5 jit_solution(5621250775307501358)
XLA Ops:
  0.6 99.3 %exchange.1 = (f32[16,192]{1,0:T(8,128)}, bf16[64,128,128]{2,1,0:T(8,128)(2,1)}) custom-call(s32[64]{0:T(128)} %tile_block.3, bf16[1,320,2304]{2,1,0:T(8,128)(2,1)} %bitcast.2, bf16[1,320,2304]{2,1,0:T(8,128)(2,1)} %factor_hbm.1, f32[16,192]{1,0:T(8,128)} %fields.1, bf16[4,48,16384]{2,1,0:T(8,128)(2,1)} %chol_hbm.1), custom_call_target="tpu_custom_call" | custom-call | tf_op jit(solution)/shard_map/exchange/pallas_call | solution.py:287
  99.9 11.5 %propagate.1 = (bf16[1,320,2304]{2,1,0:T(8,128)(2,1)}, f32[16,192]{1,0:T(8,128)}) custom-call(s32[64]{0:T(128)} %tile_block.3, bf16[64,128,128]{2,1,0:T(8,128)(2,1)} %get-tuple-element.6.parts_hbm, bf16[1,320,2304]{2,1,0:T(8,128)(2,1)} %bitcast.3, f32[16,192]{1,0:T(8,128)} %get-tuple-element.7.bias), custom_call_target="tpu_custom_call" | custom-call | tf_op jit(solution)/shard_map/propagate/pallas_call | solution.py:321

commit v5 on v3

--- a/solution.py
+++ b/solution.py
@@ -12,6 +12,8 @@
 
 step_root = 0.25
 CHUNK = 2048
+GROUP = 16
+LIMIT = 63 * 2**20
 
 
 def exchange_kernel(
@@ -23,9 +25,9 @@
     chol_hbm,
     bias_out,
     returned,
+    rows,
     chol,
     fields_here,
-    rows,
     cols,
     green,
     received,
@@ -90,7 +92,7 @@
         pltpu.make_async_remote_copy(
             src_ref=green.at[t],
             dst_ref=received.at[j, me],
-            send_sem=green_send,
+            send_sem=green_send.at[j],
             recv_sem=green_recv.at[j],
             device_id=(part, owner),
             device_id_type=MESH,
@@ -108,7 +110,12 @@
 
         return lax.fori_loop(1, half, pair, carry)
 
-    lax.fori_loop(0, tiles, send_tile, 0)
+    def sent(j):
+        others = pl.ds(0, n - 1)
+        pltpu.make_async_copy(green.at[others], green.at[others], green_send.at[j]).wait()
+
+    ahead = min(2, tiles)
+    lax.fori_loop(0, ahead, send_tile, 0)
     for j in range(tiles):
         received[j, me] = build(me * tiles + j)
     fields_copy.wait()
@@ -126,6 +133,11 @@
         ).start()
 
     def process(j, carry):
+        @pl.when(j + ahead < tiles)
+        def _():
+            sent(j)
+            send_tile(j + ahead, 0)
+
         arrived = received.at[j, pl.ds(0, n - 1)]
         pltpu.make_async_copy(arrived, arrived, green_recv.at[j]).wait()
         pltpu.make_async_copy(chol_hbm.at[j], chol.at[j], chol_sem.at[j]).wait()
@@ -175,7 +187,8 @@
         bias_out[:, j * vectors : (j + 1) * vectors] = bias_tiles[j]
 
     others = pl.ds(0, (n - 1) * tiles)
-    pltpu.make_async_copy(green.at[others], green.at[others], green_send).wait()
+    for j in range(max(tiles - ahead, 0), tiles):
+        sent(j)
     pltpu.make_async_copy(green.at[others], green.at[others], back_send).wait()
     for j in range(tiles):
         pltpu.make_async_copy(
@@ -185,17 +198,17 @@
 
 
 def propagate_kernel(
-    group, tile_block, parts, walkers, bias, out, bias_out, term, acc, total, bias_sem, out_sem
+    group, tile_block, parts, first, bias, out, bias_out, term, acc, total, bias_sem, out_sem
 ):
+    count = parts.shape[0]
+    side = term.shape[0]
     bias_copy = pltpu.make_async_copy(bias, bias_out, bias_sem)
     bias_copy.start()
-    count = parts.shape[0]
-    side = term.shape[0]
-    for r in range(side):
-        term[r] = walkers[0, :, r * BS : (r + 1) * BS]
     for order in range(1, 4):
         for r in range(side):
             acc[r] = jnp.zeros(acc.shape[1:], jnp.float32)
+
+        source = first if order == 1 else term
 
         def step(s, carry):
             for u in range(group):
@@ -204,7 +217,7 @@
                 row = lax.div(block, side)
                 col = block - row * side
                 acc[row] = acc[row] + lax.dot_general(
-                    term[col],
+                    source[col],
                     parts[t],
                     (((1,), (1,)), ((), ())),
                     preferred_element_type=jnp.float32,
@@ -215,7 +228,7 @@
         for r in range(side):
             new = (acc[r] * (-step_root) / order).astype(jnp.bfloat16)
             if order == 1:
-                before = walkers[0, :, r * BS : (r + 1) * BS].astype(jnp.float32)
+                before = first[r].astype(jnp.float32)
             else:
                 before = total[r]
             after = before + new.astype(jnp.float32)
@@ -236,23 +249,24 @@
     tiles, vectors, area = chol_tiles.shape
     all_tiles = n * tiles
     side = orbital_count // BS
-    vmem = pl.BlockSpec(memory_space=pltpu.VMEM)
     smem = pl.BlockSpec(memory_space=pltpu.SMEM)
     hbm = pl.BlockSpec(memory_space=pltpu.HBM)
-    anywhere = pl.BlockSpec(memory_space=pl.ANY)
     turned = walkers.transpose(0, 2, 1)
-    force_bias, returned = pl.pallas_call(
+    held = 2 * (all_tiles * BS * BS + orbital_count * occupied)
+    limit = LIMIT - held
+    vmem = pl.BlockSpec(memory_space=pltpu.VMEM)
+    force_bias, returned, blocks = pl.pallas_call(
         functools.partial(exchange_kernel, n),
         out_shape=(
-            jax.ShapeDtypeStruct((n, tiles * vectors), jnp.float32),
-            jax.ShapeDtypeStruct((all_tiles, BS, BS), jnp.bfloat16),
+            pltpu.VMEM((n, tiles * vectors), jnp.float32),
+            pltpu.VMEM((all_tiles, BS, BS), jnp.bfloat16),
+            pltpu.VMEM((side, occupied, BS), jnp.bfloat16),
         ),
         in_specs=[smem, hbm, hbm, hbm, hbm],
-        out_specs=(vmem, anywhere),
+        out_specs=(vmem, vmem, vmem),
         scratch_shapes=[
             pltpu.VMEM((tiles, vectors, area), jnp.bfloat16),
             pltpu.VMEM((n, tiles * vectors), jnp.float32),
-            pltpu.VMEM((side, occupied, BS), jnp.bfloat16),
             pltpu.VMEM((side, occupied, BS), jnp.bfloat16),
             pltpu.VMEM((all_tiles, BS, BS), jnp.bfloat16),
             pltpu.VMEM((tiles, n, BS, BS), jnp.bfloat16),
@@ -263,19 +277,19 @@
             pltpu.VMEM((tiles, n, vectors), jnp.float32),
             pltpu.SemaphoreType.DMA((3,)),
             pltpu.SemaphoreType.DMA((tiles,)),
-            pltpu.SemaphoreType.DMA,
+            pltpu.SemaphoreType.DMA((tiles,)),
             pltpu.SemaphoreType.DMA((tiles,)),
             pltpu.SemaphoreType.DMA,
             pltpu.SemaphoreType.DMA,
             pltpu.SemaphoreType.DMA((tiles,)),
         ],
         compiler_params=pltpu.CompilerParams(
-            collective_id=0, has_side_effects=True, vmem_limit_bytes=48 * 2**20
+            collective_id=0, has_side_effects=True, vmem_limit_bytes=limit
         ),
         name="exchange",
     )(tile_block, turned, left_factor, fields, chol_tiles)
     new_walkers, force_bias = pl.pallas_call(
-        functools.partial(propagate_kernel, 16),
+        functools.partial(propagate_kernel, GROUP),
         out_shape=(
             jax.ShapeDtypeStruct(turned.shape, jnp.bfloat16),
             jax.ShapeDtypeStruct(force_bias.shape, jnp.float32),
@@ -289,9 +303,9 @@
             pltpu.SemaphoreType.DMA,
             pltpu.SemaphoreType.DMA,
         ],
-        compiler_params=pltpu.CompilerParams(vmem_limit_bytes=48 * 2**20),
+        compiler_params=pltpu.CompilerParams(vmem_limit_bytes=24 * 2**20),
         name="propagate",
-    )(tile_block, returned, turned, force_bias)
+    )(tile_block, returned, blocks, force_bias)
     return (force_bias, new_walkers.transpose(0, 2, 1))
 
 

time: 114 us -> 109 us (0.956)
  local copies, waits for them, and re-layouts: 4.11 us -> 0.01 us
    unnamed x8 -> x2, local copies, waits for them, and re-layouts: 4.11 us -> 0.01 us
where the time goes in v5:
time: 109 us
  Pallas kernels  109 us (100%)
    pallas_call x1, Pallas kernels, per_device(): pl.pallas_call(functools.partial(exchange_kernel, n), out_shape=(pltpu.VM...  99.2 us
    pallas_call x1, Pallas kernels, per_device(): pl.pallas_call(functools.partial(propagate_kernel, GROUP), out_shape=(jax...  9.4 us

profile of v5, /device:TPU:0, one launch (start us, length us, event | category | flops | bytes accessed | tf_op | source)
XLA Modules:
  0.0 109.3 jit_solution(3182092059481657879)
XLA Ops:
  0.6 0.0 copy-start
  0.6 99.2 %exchange.1 = (f32[16,192]{1,0:T(8,128)S(1)}, bf16[64,128,128]{2,1,0:T(8,128)(2,1)S(1)}, bf16[18,320,128]{2,1,0:T(8,128)(2,1)S(1)}) custom-call(s32[64]{0:T(128)} %tile_block.3, bf16[1,320,2304]{2,1,0:T(8,128)(2,1)} %bitcast.2, bf16[1,320,2304]{2,1,0:T(8,128)(2,1)} %factor_hbm.1, f32[16,192]{1,0:T(8,128)} %fields.1, bf16[4,48,16384]{2,1,0:T(8,128)(2,1)} %chol_hbm.1), custom_call_target="tpu_custom_call" | custom-call | tf_op jit(solution)/shard_map/exchange/pallas_call | solution.py:258
  99.9 0.0 copy-done
  99.9 9.4 %propagate.1 = (bf16[1,320,2304]{2,1,0:T(8,128)(2,1)}, f32[16,192]{1,0:T(8,128)}) custom-call(s32[64]{0:T(128)S(1)} %copy-done, bf16[64,128,128]{2,1,0:T(8,128)(2,1)S(1)} %get-tuple-element.7.parts, bf16[18,320,128]{2,1,0:T(8,128)(2,1)S(1)} %get-tuple-element.8.first, f32[16,192]{1,0:T(8,128)S(1)} %get-tuple-element.9.bias), custom_call_target="tpu_custom_call" | custom-call | tf_op jit(solution)/shard_map/propagate/pallas_call | solution.py:291
Async XLA Ops:
  0.6 99.2 %copy-start = (s32[64]{0:T(128)S(1)}, s32[64]{0:T(128)}, u32[]{:S(2)}) copy-start(s32[64]{0:T(128)} %tile_block.3) | copy-start | bytes 772

commit v6 on v5

--- a/solution.py
+++ b/solution.py
@@ -12,7 +12,7 @@
 
 step_root = 0.25
 CHUNK = 2048
-GROUP = 16
+GROUP = 32
 LIMIT = 63 * 2**20
 
 
@@ -114,7 +114,7 @@
         others = pl.ds(0, n - 1)
         pltpu.make_async_copy(green.at[others], green.at[others], green_send.at[j]).wait()
 
-    ahead = min(2, tiles)
+    ahead = min(1, tiles)
     lax.fori_loop(0, ahead, send_tile, 0)
     for j in range(tiles):
         received[j, me] = build(me * tiles + j)

time: 109 us -> 108 us (level)
  no operation moved by 1% of the time
where the time goes in v6:
time: 108 us
  Pallas kernels  108 us (100%)
    pallas_call x1, Pallas kernels, per_device(): pl.pallas_call(functools.partial(exchange_kernel, n), out_shape=(pltpu.VM...  99.2 us
    pallas_call x1, Pallas kernels, per_device(): pl.pallas_call(functools.partial(propagate_kernel, GROUP), out_shape=(jax...  8.38 us

profile of v6, /device:TPU:0, one launch (start us, length us, event | category | flops | bytes accessed | tf_op | source)
XLA Modules:
  0.0 108.2 jit_solution(13267064499367681797)
XLA Ops:
  0.6 0.0 copy-start
  0.6 99.2 %exchange.1 = (f32[16,192]{1,0:T(8,128)S(1)}, bf16[64,128,128]{2,1,0:T(8,128)(2,1)S(1)}, bf16[18,320,128]{2,1,0:T(8,128)(2,1)S(1)}) custom-call(s32[64]{0:T(128)} %tile_block.3, bf16[1,320,2304]{2,1,0:T(8,128)(2,1)} %bitcast.2, bf16[1,320,2304]{2,1,0:T(8,128)(2,1)} %factor_hbm.1, f32[16,192]{1,0:T(8,128)} %fields.1, bf16[4,48,16384]{2,1,0:T(8,128)(2,1)} %chol_hbm.1), custom_call_target="tpu_custom_call" | custom-call | tf_op jit(solution)/shard_map/exchange/pallas_call | solution.py:258
  99.9 0.0 copy-done
  99.9 8.4 %propagate.1 = (bf16[1,320,2304]{2,1,0:T(8,128)(2,1)}, f32[16,192]{1,0:T(8,128)}) custom-call(s32[64]{0:T(128)S(1)} %copy-done, bf16[64,128,128]{2,1,0:T(8,128)(2,1)S(1)} %get-tuple-element.7.parts, bf16[18,320,128]{2,1,0:T(8,128)(2,1)S(1)} %get-tuple-element.8.first, f32[16,192]{1,0:T(8,128)S(1)} %get-tuple-element.9.bias), custom_call_target="tpu_custom_call" | custom-call | tf_op jit(solution)/shard_map/propagate/pallas_call | solution.py:291
Async XLA Ops:
  0.6 99.2 %copy-start = (s32[64]{0:T(128)S(1)}, s32[64]{0:T(128)}, u32[]{:S(2)}) copy-start(s32[64]{0:T(128)} %tile_block.3) | copy-start | bytes 772
